TPU v7x, 256 devices: a whole 4x4x8 slice. The times are simulated.
256 devices in a mesh: blk: 32 (over z, x_lo, core), grp: 8 (over x_hi, y).
Axes of the slice: x: 4 (x_hi: 2, x_lo: 2; x = x_hi * 2 + x_lo), y: 4, z: 8, core: 2. Of those that a mesh axis runs over, the one named last changes fastest.
Arguments:
- image_embed: bfloat16 [32768, 1152], P(('blk', 'grp')), may hold values from -0.1796875 to 0.1796875
- text_embed: bfloat16 [32768, 1152], P(('blk', 'grp')), may hold values from -0.1796875 to 0.1796875
- log_scale: float32 [1], replicated, may hold values from 1.6 to 2.6
- bias: float32 [1], replicated, may hold values from -4 to -1
Outputs:
- grad_image: float32 [32768, 1152], P(('blk', 'grp'))
- grad_text: float32 [32768, 1152], P(('blk', 'grp'))
- pair_loss: float32 [], replicated
- grad_log_scale: float32 [], replicated
- grad_bias: float32 [], replicated
All inputs are finite; a program needn't handle non-finite values.
Results may differ from a plain program's by a relative error of at most 0.0004.
The roundings to bfloat16 on the way count: a program that leaves them out, or rounds other values in their place, can miss the bound.
Values may be sent and summed in bfloat16 or wider, within the bound.
A program may use at most 128 MiB of HBM per device.

v0:
```python
import jax
import jax.numpy as jnp
from jax import lax
from jax.sharding import PartitionSpec as P

STEPS = 4


def shifted(block, axis, distance):
    devices = range(lax.axis_size(axis))
    route = [((i - distance) % len(devices), i) for i in devices]
    return lax.ppermute(block, axis, route)


def unit_rows(embed):
    wide = embed.astype(jnp.float32)
    inverse = lax.rsqrt(jnp.sum(wide * wide, axis=1, keepdims=True) + 1e-06)
    return (wide * inverse, inverse)


def text_side(weights, image_low):
    return lax.dot_general(
        weights, image_low, (((0,), (0,)), ((), ())), preferred_element_type=jnp.float32
    )


def local(image_embed, text_embed, log_scale, bias):
    rows, width = image_embed.shape
    cycle = lax.axis_size("blk")
    group = lax.axis_size("grp")
    place = lax.axis_index("blk")
    member = lax.axis_index("grp")
    block = group * rows
    image_unit, image_inv = unit_rows(image_embed)
    text_unit, text_inv = unit_rows(text_embed)
    image_low = image_unit.astype(jnp.bfloat16)
    text_low = text_unit.astype(jnp.bfloat16)
    scale = jnp.exp(log_scale[0])
    offset = bias[0]
    row_ids = (place * group + member) * rows + jnp.arange(rows, dtype=jnp.int32)
    within = jnp.arange(block, dtype=jnp.int32)
    image_back = jnp.zeros((rows, width), jnp.float32)
    loss_sum = jnp.float32(0.0)
    scale_sum = jnp.float32(0.0)
    bias_sum = jnp.float32(0.0)
    texts = lax.all_gather(text_low, "grp", axis=0, tiled=True)
    carried = jnp.zeros((block, width), jnp.float32)
    for step in range(STEPS):
        if step > 0:
            texts = shifted(texts, "blk", 1)
        anchor = (place - step) % cycle
        col_ids = anchor * block + within
        logits = lax.dot_general(
            image_low, texts, (((1,), (1,)), ((), ())), preferred_element_type=jnp.float32
        )
        label = jnp.where(row_ids[:, None] == col_ids[None, :], 1.0, -1.0).astype(jnp.float32)
        score = scale * logits + offset
        loss = jnp.sum(jax.nn.softplus(-label * score))
        slope = -label * jax.nn.sigmoid(-label * score)
        dscale = jnp.sum(slope * logits) * scale
        dbias = jnp.sum(slope)
        weights = (scale * slope).astype(jnp.bfloat16)
        dimage = jnp.dot(weights, texts, preferred_element_type=jnp.float32)
        weights, dimage, loss, dscale, dbias = (weights, dimage, loss, dscale, dbias)
        image_back = image_back + dimage
        loss_sum = loss_sum + loss
        scale_sum = scale_sum + dscale
        bias_sum = bias_sum + dbias
        carried = carried + text_side(weights, image_low)
        if step < STEPS - 1:
            carried = shifted(carried, "blk", 1)
    finished = lax.psum_scatter(carried, "grp", scatter_dimension=0, tiled=True)
    text_back = shifted(finished, "blk", -(STEPS - 1))
    grad_image = image_inv * (
        image_back - image_unit * jnp.sum(image_unit * image_back, axis=1, keepdims=True)
    )
    grad_text = text_inv * (
        text_back - text_unit * jnp.sum(text_unit * text_back, axis=1, keepdims=True)
    )
    total_loss, total_scale, total_bias = lax.psum((loss_sum, scale_sum, bias_sum), ("blk", "grp"))
    pairs = float(cycle * block * STEPS * block)
    return (grad_image, grad_text, total_loss / pairs, total_scale / pairs, total_bias / pairs)


def solution(mesh):
    in_specs = (P(("blk", "grp"), None), P(("blk", "grp"), None), P(), P())
    out_specs = (P(("blk", "grp"), None), P(("blk", "grp"), None), P(), P(), P())
    return jax.shard_map(local, mesh=mesh, in_specs=in_specs, out_specs=out_specs, check_vma=False)
```

profile of v0, /device:TPU:1, one launch (start us, length us, event | category | flops | bytes accessed | tf_op | source)
XLA Modules:
  0.0 538.7 jit_solution(5288281335805063160)
XLA Ops:
  7.2 0.0 copy-start
  7.2 0.0 all-gather.2.cloned.1.call-start
  7.2 1.1 fusion.13
  8.4 1.8 fusion.2
  10.2 0.0 all-gather.2.cloned.1.call-update
  10.2 0.0 reduce-scatter.2.cloned.1.call-start
  11.6 1.1 fusion.9
  12.7 63.0 %all-gather.2.cloned.1.call-done = bf16[1024,1152]{1,0:T(8,128)(2,1)} async-done(((bf16[128,1152]{1,0:T(8,128)(2,1)}), bf16[1024,1152]{1,0:T(8,128)(2,1)}) %all-gather.2.cloned.1.call-update) | async-done | bytes 2359312 | tf_op jit(solution)/shard_map/all_gather | solution.py:46
  75.7 2.7 fusion.32
  78.4 0.0 copy-done
  78.4 0.0 copy-start.2
  78.4 3.2 fusion.18
  81.5 1.3 collective-permute-start.3
  82.8 0.0 copy-done.2
  82.8 0.0 collective-permute-start
  82.8 76.5 %collective-permute-done = bf16[1024,1152]{1,0:T(8,128)(2,1)} collective-permute-done((bf16[1024,1152]{1,0:T(8,128)(2,1)S(1)}, bf16[1024,1152]{1,0:T(8,128)(2,1)}, u32[]{:S(2)}, u32[]{:S(2)}) %collective-permute-start) | collective-permute-done | bytes 2359328 | tf_op jit(solution)/shard_map/ppermute | solution.py:12
  159.3 2.6 fusion.30
  161.9 0.0 copy-start.5
  161.9 0.0 collective-permute-done.3
  161.9 5.7 %convolution_add_fusion = f32[1024,1152]{1,0:T(8,128)} fusion(f32[1024,1152]{1,0:T(8,128)} %collective-permute-done.3, f32[]{:T(128)} %bitcast, bf16[128,1152]{1,0:T(8,128)(2,1)S(1)} %copy-done, f32[128]{0:T(128)S(1)} %add_rsqrt_fusion.1, f32[128,1024]{1,0:T(8,128)S(1)} %fusion.30, s32[1024]{0:T(1024)S(1)} %iota_add_fusion.2, f32[]{:T(128)} %bitcast.14, ...), kind=kOutput, calls=%fused_computation | convolution fusion | flops 305184768 | bytes 10261512 | tf_op jit(solution)/shard_map/dot_general | solution.py:22
  167.6 0.0 copy-done.5
  167.6 2.6 collective-permute-start.4
  170.2 0.0 collective-permute-start.1
  170.3 76.6 %collective-permute-done.1 = bf16[1024,1152]{1,0:T(8,128)(2,1)} collective-permute-done((bf16[1024,1152]{1,0:T(8,128)(2,1)}, bf16[1024,1152]{1,0:T(8,128)(2,1)}, u32[]{:S(2)}, u32[]{:S(2)}) %collective-permute-start.1) | collective-permute-done | bytes 2359328 | tf_op jit(solution)/shard_map/ppermute | solution.py:12
  246.9 2.5 fusion.28
  249.4 0.0 copy-start.3
  249.4 1.0 fusion.20
  250.5 0.0 copy-done.3
  250.5 0.0 collective-permute-done.4
  250.5 4.9 add.211
  255.4 2.5 collective-permute-start.5
  257.9 1.0 collective-permute-start.2
  258.9 75.7 %collective-permute-done.2 = bf16[1024,1152]{1,0:T(8,128)(2,1)} collective-permute-done((bf16[1024,1152]{1,0:T(8,128)(2,1)}, bf16[1024,1152]{1,0:T(8,128)(2,1)}, u32[]{:S(2)}, u32[]{:S(2)}) %collective-permute-start.2) | collective-permute-done | bytes 2359328 | tf_op jit(solution)/shard_map/ppermute | solution.py:12
  334.5 5.5 %fusion.37 = (f32[]{:T(128)}, f32[]{:T(128)}, f32[]{:T(128)}, f32[]{:T(128)}, f32[]{:T(128)}, /*index=5*/f32[]{:T(128)}, f32[]{:T(128)}, f32[]{:T(128)}, f32[]{:...) fusion(f32[]{:T(128)} %bitcast.11, f32[]{:T(128)} %bitcast, s32[1024]{0:T(1024)S(1)} %iota_add_fusion, ...), kind=kOutput, calls=%fused_computation.68 | convolution fusion | flops 312918016 | bytes 4768824 | tf_op jit(solution)/shard_map/dot_general | solution.py:53
  340.1 0.0 copy-start.7
  340.1 1.0 fusion.21
  341.1 0.0 copy-done.7
  341.1 0.0 collective-permute-done.5
  341.1 4.9 add.212
  346.0 0.0 reduce-scatter.2.cloned.1.call-update
  346.0 0.0 copy-start.6
  346.1 0.7 fusion.19
  346.7 0.4 copy-done.6
  347.1 0.0 copy-start.4
  347.1 2.4 convolution_add_fusion.3
  349.5 0.0 copy-done.4
  349.5 0.0 copy-start.8
  349.5 2.4 convolution_add_fusion.2
  359.3 84.1 %reduce-scatter.2.cloned.1.call-done = f32[128,1152]{1,0:T(8,128)} async-done(((f32[1024,1152]{1,0:T(8,128)}), f32[128,1152]{1,0:T(8,128)}) %reduce-scatter.2.cloned.1.call-update) | async-done | bytes 589840 | tf_op jit(solution)/shard_map/reduce_scatter | solution.py:72
  443.5 4.6 collective-permute-start.6
  448.0 0.0 copy-done.8
  448.1 0.0 copy-start.1
  448.1 2.5 fusion.6
  450.5 73.7 %all-reduce = (f32[]{:T(128)}, f32[]{:T(128)}, f32[]{:T(128)}) all-reduce(f32[]{:T(128)S(6)} %add.219, f32[]{:T(128)S(6)} %multiply.5, f32[]{:T(128)S(6)} %add.225), channel_id=1, replica_groups=mesh['blk'=32,'grp'=8] {'blk','grp'}, use_global_device_ids=true, to_apply=%region_9.10 | all-reduce | flops 3 | bytes 24 | tf_op jit(solution)/shard_map/psum | solution.py:80
  526.1 1.0 fusion.8
  527.1 0.0 collective-permute-done.6
  527.2 0.0 copy-done.1
  527.2 0.2 fusion.10
  527.4 1.0 fusion.12
  (7 shorter events, 0.0 us)
Async XLA Ops:
  7.2 71.2 %copy-start = (bf16[128,1152]{1,0:T(8,128)(2,1)S(1)}, bf16[128,1152]{1,0:T(8,128)(2,1)}, u32[]{:S(2)}) copy-start(bf16[128,1152]{1,0:T(8,128)(2,1)} %param.4) | copy-start | bytes 884740
  7.2 68.5 %all-gather.2.cloned.1.call-start = ((), (), s32[]{:S(2)}) async-start(), calls=%async_computation.1 | async-start | bytes 2654208 | tf_op jit(solution)/shard_map/all_gather | solution.py:46
  10.2 433.3 %reduce-scatter.2.cloned.1.call-start = ((), (), s32[]{:S(2)}) async-start(), calls=%async_computation.2 | async-start | bytes 5308416 | tf_op jit(solution)/shard_map/reduce_scatter | solution.py:72
  78.4 4.4 copy-start.2
  81.5 80.4 %collective-permute-start.3 = (f32[1024,1152]{1,0:T(8,128)}, f32[1024,1152]{1,0:T(8,128)}, u32[]{:S(2)}, u32[]{:S(2)}) collective-permute-start(f32[1024,1152]{1,0:T(8,128)} %fusion.18), channel_id=1, source_target_pairs={{248,0},{0,8},{8,16},{16,24},{24,32},{32,40},{40,48},{48,56},{56,6... | collective-permute-start | bytes 14155784 | tf_op jit(solution)/shard_map/ppermute | solution.py:12
  82.8 76.6 %collective-permute-start = (bf16[1024,1152]{1,0:T(8,128)(2,1)S(1)}, bf16[1024,1152]{1,0:T(8,128)(2,1)}, u32[]{:S(2)}, u32[]{:S(2)}) collective-permute-start(bf16[1024,1152]{1,0:T(8,128)(2,1)S(1)} %copy-done.2), channel_id=1, source_target_pairs={{248,0},{0,8},{8,16},{16,24},{24,32},{32,40},{40,48},{48,56},{56,6... | collective-permute-start | bytes 7077896 | tf_op jit(solution)/shard_map/ppermute | solution.py:12
  161.9 5.7 %copy-start.5 = (f32[128,1024]{1,0:T(8,128)}, f32[128,1024]{1,0:T(8,128)S(1)}, u32[]{:S(2)}) copy-start(f32[128,1024]{1,0:T(8,128)S(1)} %fusion.30) | copy-start | bytes 1572868
  167.6 82.8 %collective-permute-start.4 = (f32[1024,1152]{1,0:T(8,128)}, f32[1024,1152]{1,0:T(8,128)}, u32[]{:S(2)}, u32[]{:S(2)}) collective-permute-start(f32[1024,1152]{1,0:T(8,128)} %convolution_add_fusion), channel_id=1, source_target_pairs={{248,0},{0,8},{8,16},{16,24},{24,32},{32,40},{40,48},{48,56},{56,6... | collective-permute-start | bytes 14155784 | tf_op jit(solution)/shard_map/ppermute | solution.py:12
  170.2 76.7 %collective-permute-start.1 = (bf16[1024,1152]{1,0:T(8,128)(2,1)}, bf16[1024,1152]{1,0:T(8,128)(2,1)}, u32[]{:S(2)}, u32[]{:S(2)}) collective-permute-start(bf16[1024,1152]{1,0:T(8,128)(2,1)} %collective-permute-done), channel_id=1, source_target_pairs={{248,0},{0,8},{8,16},{16,24},{24,32},{32,40},{40,48},{48,56},{56,6... | collective-permute-start | bytes 7077896 | tf_op jit(solution)/shard_map/ppermute | solution.py:12
  249.4 1.0 copy-start.3
  255.4 85.7 %collective-permute-start.5 = (f32[1024,1152]{1,0:T(8,128)}, f32[1024,1152]{1,0:T(8,128)}, u32[]{:S(2)}, u32[]{:S(2)}) collective-permute-start(f32[1024,1152]{1,0:T(8,128)} %add.211), channel_id=1, source_target_pairs={{248,0},{0,8},{8,16},{16,24},{24,32},{32,40},{40,48},{48,56},{56,6... | collective-permute-start | bytes 14155784 | tf_op jit(solution)/shard_map/ppermute | solution.py:12
  257.9 76.7 %collective-permute-start.2 = (bf16[1024,1152]{1,0:T(8,128)(2,1)}, bf16[1024,1152]{1,0:T(8,128)(2,1)}, u32[]{:S(2)}, u32[]{:S(2)}) collective-permute-start(bf16[1024,1152]{1,0:T(8,128)(2,1)} %collective-permute-done.1), channel_id=1, source_target_pairs={{248,0},{0,8},{8,16},{16,24},{24,32},{32,40},{40,48},{48,56},{56,6... | collective-permute-start | bytes 7077896 | tf_op jit(solution)/shard_map/ppermute | solution.py:12
  340.1 1.0 copy-start.7
  346.0 1.0 copy-start.6
  347.1 2.4 copy-start.4
  349.5 98.6 %copy-start.8 = (f32[128,1024]{1,0:T(8,128)S(1)}, f32[128,1024]{1,0:T(8,128)}, u32[]{:S(2)}) copy-start(f32[128,1024]{1,0:T(8,128)} %copy-done.7) | copy-start | bytes 1572868
  443.5 83.7 %collective-permute-start.6 = (f32[128,1152]{1,0:T(8,128)}, f32[128,1152]{1,0:T(8,128)S(1)}, u32[]{:S(2)}, u32[]{:S(2)}) collective-permute-start(f32[128,1152]{1,0:T(8,128)} %reduce-scatter.2.cloned.1.call-done), channel_id=1, source_target_pairs={{24,0},{32,8},{40,16},{48,24},{56,32},{64,40},{72,48},{80,56},{88,... | collective-permute-start | bytes 1769480 | tf_op jit(solution)/shard_map/ppermute | solution.py:12
  448.1 79.1 %copy-start.1 = (bf16[128,1152]{1,0:T(8,128)(2,1)S(1)}, bf16[128,1152]{1,0:T(8,128)(2,1)}, u32[]{:S(2)}) copy-start(bf16[128,1152]{1,0:T(8,128)(2,1)} %param.5) | copy-start | bytes 884740
Sparse Core Ops, SparseCore 0:
  11.2 64.4 all-gather.1
  346.2 97.2 reduce-scatter.1
where the time goes:
time: 539 us
  waiting for transfers between devices  376 us (70%)
  blocking collectives  73.7 us (14%)
  matrix products  32 us (6%)
  between operations  28.3 us (5%)
  other arithmetic  16.2 us (3%)
  starting transfers between devices  12.1 us (2%)
    ppermute x7, waiting for transfers between devices, shifted(): return lax.ppermute(block, axis, route)  229 us
    reduce_scatter x1, waiting for transfers between devices, local(): finished = lax.psum_scatter(carried, 'grp', scatter_dimension=0, tiled=True)  84.1 us
    psum x1, blocking collectives, local(): lax.psum((loss_sum, scale_sum, bias_sum), ('blk', 'grp'))  73.7 us
    all_gather x1, waiting for transfers between devices, local(): texts = lax.all_gather(text_low, 'grp', axis=0, tiled=True)  63 us
    dot_general x4, matrix products, local(): lax.dot_general(image_low, texts, (((1,), (1,)), ((), ())), preferred_ele...  13.3 us
    ppermute x7, starting transfers between devices, shifted(): return lax.ppermute(block, axis, route)  12 us
    dot_general x4, matrix products, text_side(): lax.dot_general(weights, image_low, (((0,), (0,)), ((), ())), preferred_e...  10.8 us
  transfers between devices with their start and end apart: 9, of which 5 were waited for; matrix products, arithmetic and copies ran while one was open for 4% of the time, Pallas kernels for 0%

commit v1 on v0

v1 whole, which is shorter than its diff:
```python
import functools

import jax
import jax.numpy as jnp
from jax import lax
from jax.experimental import pallas as pl
from jax.experimental.pallas import tpu as pltpu
from jax.sharding import PartitionSpec as P

MESH = pl.DeviceIdType.MESH
STEPS = 4
NT = (((1,), (1,)), ((), ()))
TN = (((0,), (0,)), ((), ()))
NN = (((1,), (0,)), ((), ()))


def normalize(embed):
    wide = embed.astype(jnp.float32)
    inverse = lax.rsqrt(jnp.sum(wide * wide, axis=1, keepdims=True) + 1e-06)
    return wide * inverse, inverse


def finish(embed, back):
    unit, inverse = normalize(embed)
    return inverse * (back - unit * jnp.sum(unit * back, axis=1, keepdims=True))


def dot(a, b, dims):
    return lax.dot_general(a, b, dims, preferred_element_type=jnp.float32)


def kernel(
    n_blk, n_grp,
    scale_ref, bias_ref, image_ref, text_ref,
    grad_image_ref, grad_text_ref, sums_ref,
    images, texts, own_text, scores, weights, text_part, image_part, image_other,
    core_in, image_in, text_in, acc, sums_in,
    image_send, image_recv, share_send, share_recv, text_send, text_recv,
    tgrad_send, tgrad_recv, core_send, core_recv, igrad_send, igrad_recv, sum_send, sum_recv,
):
    rows = image_ref.shape[0]
    p = lax.axis_index("blk")
    g = lax.axis_index("grp")
    c = lax.rem(p, 2)
    base = p - c
    h = g // 4
    y = lax.rem(g, 4)
    sibling = (base + 1 - c, g)

    def ring(blk):
        return lax.rem(blk + n_blk, n_blk)

    def along_y(d):
        return (p, h * 4 + lax.rem(y + d + 4, 4))

    def user(m, hh):
        return (ring(base + 2 * m + h), hh * 4 + y)

    def owner(s):
        return (ring(base - 3 + s), c * 4 + y)

    def each_user(action):
        for m in range(3):
            for hh in range(2):
                here = (c == h) & (h == hh) if m == 0 else False
                there = m < 2 + c
                if m == 0:
                    pl.when(jnp.logical_not(here))(functools.partial(action, m, hh))
                else:
                    pl.when(there)(functools.partial(action, m, hh))

    def each_owner(action):
        for s in range(5):
            if s < 3:
                action(s)
            else:
                mine = (c == h) & (c == s - 3)
                pl.when(jnp.logical_not(mine))(functools.partial(action, s))

    barrier = pltpu.get_barrier_semaphore()

    def greet(device):
        pl.semaphore_signal(barrier, inc=1, device_id=device, device_id_type=MESH)

    for d in (1, 2, 3):
        greet(along_y(d))
    greet(sibling)
    each_user(lambda m, hh: greet(user(m, hh)))
    each_owner(lambda s: greet(owner(s)))
    rounds = [("blk", 1 << r) for r in range(5)] + [("grp", 1 << r) for r in range(3)]

    def partner(r):
        axis, bit = rounds[r]
        if axis == "blk":
            flip = lax.rem(p // bit, 2)
            return (p + bit - 2 * bit * flip, g)
        flip = lax.rem(g // bit, 2)
        return (p, g + bit - 2 * bit * flip)

    for r in range(8):
        greet(partner(r))

    own_low = normalize(image_ref[...])[0].astype(jnp.bfloat16)
    images[c, 0] = own_low
    own_text[...] = normalize(text_ref[...])[0].astype(jnp.bfloat16)
    acc[...] = jnp.zeros_like(acc)

    mine = (c == h).astype(jnp.int32)
    pl.semaphore_wait(barrier, 3 + 1 + 8 + 5 - mine + 2 * (2 + c) - mine)

    def remote(src, dst, send, recv, device):
        return pltpu.make_async_remote_copy(
            src_ref=src, dst_ref=dst, send_sem=send, recv_sem=recv, device_id=device, device_id_type=MESH
        )

    def text_copy(m, hh):
        slot = 3 + c - 2 * m if m < 2 else 0
        return remote(own_text, texts.at[slot], text_send.at[m, hh], text_recv.at[slot], user(m, hh))

    def text_arrival(s):
        return remote(own_text, texts.at[s], text_send.at[0, 0], text_recv.at[s], sibling)

    def image_copy(d):
        slot = (4 - d) % 4
        return remote(images.at[c, 0], images.at[c, slot], image_send.at[d], image_recv.at[slot], along_y(d))

    def share(slot):
        return remote(images.at[c, slot], images.at[c, slot], share_send.at[slot], share_recv.at[slot], sibling)

    for d in (1, 3, 2):
        image_copy(d).start()
    share(0).start()
    each_user(lambda m, hh: text_copy(m, hh).start())

    @pl.when(c == h)
    def _():
        texts[3 + c] = own_text[...]

    for slot in (1, 3, 2):
        image_copy(4 - slot).wait_recv()
        share(slot).start()
    for slot in (0, 1, 3, 2):
        remote(images.at[c, slot], images.at[1 - c, slot], share_send.at[slot], share_recv.at[slot], sibling).wait_recv()

    scale = jnp.exp(scale_ref[0])
    offset = bias_ref[0]
    eye = lax.broadcasted_iota(jnp.int32, (rows, rows), 0) == lax.broadcasted_iota(jnp.int32, (rows, rows), 1)

    def logistic(score):
        small = jnp.exp(-jnp.abs(score))
        whole = 1.0 + small
        inverse = 1.0 / whole
        loss = jnp.maximum(score, 0.0) + (jnp.log(whole) + (small - (whole - 1.0)) * inverse)
        return loss, jnp.where(score >= 0.0, 1.0, small) * inverse

    def tile(s, b, yy, paired):
        logits = scores[:, pl.ds(pl.multiple_of(yy * rows, rows), rows)]
        score = scale * logits + offset
        if paired is None:
            loss, slope = logistic(score)
        else:
            match = eye & paired
            loss, slope = logistic(jnp.where(match, -score, score))
            slope = jnp.where(match, -slope, slope)
        weights[s, b, yy] = (scale * slope).astype(jnp.bfloat16)
        acc[0] += loss.reshape(-1, 8, rows).sum(axis=0)
        acc[1] += (slope * logits).reshape(-1, 8, rows).sum(axis=0)
        acc[2] += slope.reshape(-1, 8, rows).sum(axis=0)

    width = image_ref.shape[1]

    def half(s, b, add):
        block = images[b].reshape(4 * rows, width)
        scores[...] = dot(texts[s], block, NT)
        tile(s, b, 0, (c == h) & (s == 3 + b))

        def body(yy, carry):
            tile(s, b, yy, None)
            return carry

        lax.fori_loop(1, 4, body, 0)
        part = sum(
            dot(weights[s, b, yy], images[b, yy], NN) for yy in range(4)
        )
        if add:
            text_part[s] += part
        else:
            text_part[s] = part

    def tgrad_copy(s):
        m = (4 + c - s) // 2 if isinstance(s, int) else (4 + c - s) // 2
        return m

    def send_part(s):
        m = {0: 2, 1: 1, 2: 1, 3: 0, 4: 0}[s]
        return remote(text_part.at[s], text_in.at[m, h], tgrad_send.at[s], tgrad_recv.at[m, h], owner(s))

    def start_part(s):
        if s < 3:
            send_part(s).start()
        else:
            mine = (c == h) & (c == s - 3)

            @pl.when(jnp.logical_not(mine))
            def _():
                send_part(s).start()

    for s in (3, 4, 2, 1, 0):
        if s >= 3:
            mine = (c == h) & (c == s - 3)
            pl.when(jnp.logical_not(mine))(lambda s=s: text_arrival(s).wait_recv())
        else:
            text_arrival(s).wait_recv()
        if s < 4:
            half(s, 0, False)
        if s > 0:
            half(s, 1, s < 4)
        start_part(s)

    def image_sum(b, yy):
        lhs = weights[pl.ds(b, 4), b, yy].reshape(4 * rows, rows)
        rhs = texts[pl.ds(b, 4)].reshape(4 * rows, width)
        return dot(lhs, rhs, TN)

    def core_copy(slot):
        return remote(image_other.at[slot], core_in.at[slot], core_send.at[slot], core_recv.at[slot], sibling)

    def igrad_copy(slot):
        return remote(image_part.at[slot], image_in.at[4 - slot], igrad_send.at[slot], igrad_recv.at[4 - slot], along_y(slot))

    for slot in (2, 1, 3, 0):
        image_other[slot] = image_sum(1 - c, slot)
        core_copy(slot).start()
    for slot in (2, 1, 3, 0):
        image_part[slot] = image_sum(c, slot)
        core_copy(slot).wait_recv()
        image_part[slot] += core_in[slot]
        if slot:
            igrad_copy(slot).start()

    sums_in[8, 0] = jnp.sum(acc[0], axis=0, keepdims=True)
    sums_in[8, 1] = jnp.sum(acc[1], axis=0, keepdims=True)
    sums_in[8, 2] = jnp.sum(acc[2], axis=0, keepdims=True)
    for r in range(8):
        copy = remote(sums_in.at[8 + r], sums_in.at[r], sum_send.at[r], sum_recv.at[r], partner(r))
        copy.start()
        copy.wait_recv()
        sums_in[9 + r] = sums_in[8 + r] + sums_in[r]
    total = jnp.sum(sums_in[16], axis=-1, keepdims=True)
    pairs = float(n_blk * n_grp * rows * STEPS * n_grp * rows)
    sums_ref[0:1, :] = jnp.broadcast_to(total[0] / pairs, (1, 128))
    sums_ref[1:2, :] = jnp.broadcast_to(total[1] * scale / pairs, (1, 128))
    sums_ref[2:3, :] = jnp.broadcast_to(total[2] / pairs, (1, 128))

    text_back = jnp.where((c == h), 1.0, 0.0)
    del text_back

    def tgrad_arrival(m, hh):
        remote(text_part.at[0], text_in.at[m, hh], tgrad_send.at[0], tgrad_recv.at[m, hh], sibling).wait_recv()

    each_user(tgrad_arrival)

    @pl.when(c == h)
    def _():
        text_in[0, h] = text_part[3 + c]

    @pl.when(c == 0)
    def _():
        text_in[2, 0] = jnp.zeros_like(text_in[2, 0])
        text_in[2, 1] = jnp.zeros_like(text_in[2, 1])

    text_back = text_in[0, 0] + text_in[0, 1] + text_in[1, 0] + text_in[1, 1] + text_in[2, 0] + text_in[2, 1]
    grad_text_ref[...] = finish(text_ref[...], text_back)

    for slot in (1, 3, 2):
        igrad_copy(4 - slot).wait_recv()
    image_back = image_part[0] + image_in[1] + image_in[2] + image_in[3]
    grad_image_ref[...] = finish(image_ref[...], image_back)

    for d in (1, 2, 3):
        image_copy(d).wait_send()
        igrad_copy(d).wait_send()
    for slot in range(4):
        share(slot).wait_send()
        core_copy(slot).wait_send()
    each_user(lambda m, hh: text_copy(m, hh).wait_send())
    each_owner(lambda s: send_part(s).wait_send())
    for r in range(8):
        remote(sums_in.at[8 + r], sums_in.at[r], sum_send.at[r], sum_recv.at[r], partner(r)).wait_send()


def local(n_blk, n_grp, image_embed, text_embed, log_scale, bias):
    rows, width = image_embed.shape
    low, wide = jnp.bfloat16, jnp.float32
    dma = pltpu.SemaphoreType.DMA
    vmem = pl.BlockSpec(memory_space=pltpu.VMEM)
    smem = pl.BlockSpec(memory_space=pltpu.SMEM)
    out = jax.ShapeDtypeStruct((rows, width), wide)
    pairs = n_grp * rows * STEPS * rows
    grad_image, grad_text, sums = pl.pallas_call(
        functools.partial(kernel, n_blk, n_grp),
        out_shape=(out, out, jax.ShapeDtypeStruct((8, 128), wide)),
        in_specs=[smem, smem, vmem, vmem],
        out_specs=(vmem, vmem, vmem),
        scratch_shapes=[
            pltpu.VMEM((2, 4, rows, width), low),
            pltpu.VMEM((5, rows, width), low),
            pltpu.VMEM((rows, width), low),
            pltpu.VMEM((rows, 4 * rows), wide),
            pltpu.VMEM((5, 2, 4, rows, rows), low),
            pltpu.VMEM((5, rows, width), wide),
            pltpu.VMEM((4, rows, width), wide),
            pltpu.VMEM((4, rows, width), wide),
            pltpu.VMEM((4, rows, width), wide),
            pltpu.VMEM((4, rows, width), wide),
            pltpu.VMEM((3, 2, rows, width), wide),
            pltpu.VMEM((3, 8, 128), wide),
            pltpu.VMEM((17, 3, 1, 128), wide),
            dma((4,)), dma((4,)), dma((4,)), dma((4,)), dma((3, 2)), dma((5,)),
            dma((5,)), dma((3, 2)), dma((4,)), dma((4,)), dma((4,)), dma((4,)), dma((8,)), dma((8,)),
        ],
        compiler_params=pltpu.CompilerParams(
            collective_id=0, has_side_effects=True, vmem_limit_bytes=48 << 20
        ),
        cost_estimate=pl.CostEstimate(
            flops=6 * pairs * width, bytes_accessed=12 * rows * width, transcendentals=3 * pairs
        ),
        name="pair_loss",
    )(log_scale, bias, image_embed, text_embed)
    return grad_image, grad_text, sums[0, 0], sums[1, 0], sums[2, 0]


def solution(mesh):
    split = P(("blk", "grp"), None)
    return jax.shard_map(
        functools.partial(local, mesh.shape["blk"], mesh.shape["grp"]),
        mesh=mesh,
        in_specs=(split, split, P(), P()),
        out_specs=(split, split, P(), P(), P()),
        check_vma=False,
    )
```

time: 539 us -> 95.8 us (0.18)
  the two profiles are of different devices: /device:TPU:1 before, /device:TPU:24 now
where the time goes in v1:
time: 95.8 us; the launch traced here: 95.6 us
  Pallas kernels  89.6 us (94%)
  local copies, waits for them, and re-layouts  4.07 us (4%)
  between operations  1.94 us (2%)
    pallas_call x1, Pallas kernels, local(): pl.pallas_call(functools.partial(kernel, n_blk, n_grp), out_shape=(out, o...  89.6 us
    unnamed x6, local copies, waits for them, and re-layouts  3.54 us

profile of v1, /device:TPU:24, one launch (start us, length us, event | category | flops | bytes accessed | tf_op | source)
XLA Modules:
  0.0 95.6 jit_solution(15740149094348048571)
XLA Ops:
  1.9 0.0 copy-start
  1.9 1.0 copy-done
  2.9 0.0 copy-start.1
  2.9 1.0 %copy-done.1 = bf16[128,1152]{1,0:T(8,128)(2,1)S(1)} copy-done((bf16[128,1152]{1,0:T(8,128)(2,1)S(1)}, bf16[128,1152]{1,0:T(8,128)(2,1)}, u32[]{:S(2)}) %copy-start.1) | copy-done | bytes 294936
  3.8 89.6 %pair_loss.1 = (f32[128,1152]{1,0:T(8,128)S(1)}, f32[128,1152]{1,0:T(8,128)S(1)}, f32[8,128]{1,0:T(8,128)S(1)}) custom-call(f32[1]{0:T(128)S(6)} %copy.11.scale_ref, f32[1]{0:T(128)S(6)} %copy.12.bias_ref, bf16[128,1152]{1,0:T(8,128)(2,1)S(1)} %copy-done, bf16[128,1152]{1,0:T(8,128)(2,1)S(1)} %copy-done.1), custom_call_target="tpu_custom_call" | custom-call | flops 3623878656 | bytes 1769472 | tf_op jit(solution)/shard_map/pair_loss/pallas_call | solution.py:300
  93.4 0.5 fusion
  94.0 0.8 copy.13
  94.8 0.8 copy.14
Async XLA Ops:
  1.9 1.0 %copy-start = (bf16[128,1152]{1,0:T(8,128)(2,1)S(1)}, bf16[128,1152]{1,0:T(8,128)(2,1)}, u32[]{:S(2)}) copy-start(bf16[128,1152]{1,0:T(8,128)(2,1)} %image_ref.1) | copy-start | bytes 884740
  2.9 1.0 %copy-start.1 = (bf16[128,1152]{1,0:T(8,128)(2,1)S(1)}, bf16[128,1152]{1,0:T(8,128)(2,1)}, u32[]{:S(2)}) copy-start(bf16[128,1152]{1,0:T(8,128)(2,1)} %text_ref.1) | copy-start | bytes 884740

commit v2 on v0

v2 whole, which is shorter than its diff:
```python
import functools

import jax
import jax.numpy as jnp
from jax import lax
from jax.experimental import pallas as pl
from jax.experimental.pallas import tpu as pltpu
from jax.sharding import PartitionSpec as P

MESH = pl.DeviceIdType.MESH
STEPS = 4
ROUND = 12582912.0
NT = (((1,), (1,)), ((), ()))
TN = (((0,), (0,)), ((), ()))
NN = (((1,), (0,)), ((), ()))

ORDER = ((2, 1, 0, 3), (1, 0, 1, 0), (0, 2, 3, 2), (3, 3, 2, 4), (4, 4, 4, 1))
PART_Z = ((-1, 0, -1, 0), (0, 0, -1, -1), (-1, 0, 0, 0), (0, 0, 0, 0), (0, 0, 0, 0))
PART_X = ((0, -1, 0, -1), (1, 0, 0, 0), (0, 0, 1, 1), (0, 0, -1, 0), (0, 0, 0, 0))
PART_CORE = ((2, 0, 2, 2), (2, 2, 2, 2), (1, 2, 2, 1), (0, 0, 2, 2), (1, 1, 2, 2))
PART_SLOT = ((1, 4, 0, 2), (1, 0, 1, 0), (6, 0, 1, 5), (3, 3, 0, 0), (3, 3, 0, 0))
SENT = ((1, 1, 1, 1), (1, 0, 1, 1), (1, 0, 1, 1), (2, 2, 1, 0), (3, 3, 0, 0))


def normalize(embed):
    wide = embed.astype(jnp.float32)
    inverse = lax.rsqrt(jnp.sum(wide * wide, axis=1, keepdims=True) + 1e-06)
    return wide * inverse, inverse


def finish(embed, back):
    unit, inverse = normalize(embed)
    return inverse * (back - unit * jnp.sum(unit * back, axis=1, keepdims=True))


def encode(value):
    top = jnp.max(jnp.abs(value), axis=1, keepdims=True)
    step = (jnp.maximum(top, 1e-30) * (1.008 / 16383.0)).astype(jnp.bfloat16).astype(jnp.float32)
    whole = (value * (1.0 / step) + ROUND) - ROUND
    upper = jnp.floor(whole * (1.0 / 128.0))
    lower = whole - 128.0 * upper
    signed = jnp.where(upper >= 0.0, upper + 128.0, upper - 127.0)
    return (signed * jnp.exp2(lower - 71.0)).astype(jnp.bfloat16), step.astype(jnp.bfloat16)


def decode(code, step):
    wide = code.astype(jnp.float32)
    size = jnp.abs(wide)
    power = jnp.floor(jnp.log2(size) + 0.001)
    mantissa = size * jnp.exp2(7.0 - power)
    upper = jnp.where(wide >= 0.0, mantissa - 128.0, 127.0 - mantissa)
    return (upper * 128.0 + (power + 64.0)) * step.astype(jnp.float32)


def dot(a, b, dims):
    return lax.dot_general(a, b, dims, preferred_element_type=jnp.float32)


def kernel(
    n_blk, n_grp,
    scale_ref, bias_ref, image_hbm, text_hbm,
    grad_image_ref, grad_text_ref, sums_ref,
    image_ref, text_ref, load_sem, images, texts, own_text, scores, weights, parts, wires, inbox, late_wires,
    image_part, image_other, core_in, back_wires, relay, image_in, acc, totals,
    ring_send, ring_recv, share_send, share_recv, first_send, hand_send, text_recv,
    part_send, late_send, part_recv, core_send, core_recv, back_send, relay_recv, image_recv,
    total_send, total_recv,
):
    rows, width = image_ref.shape
    chunk = rows // 2
    p = lax.axis_index("blk")
    g = lax.axis_index("grp")
    c = lax.rem(p, 2)
    z = p // 4
    low = lax.rem(p // 2, 2)
    h = g // 4
    y = lax.rem(g, 4)
    x = 2 * h + low
    role = lax.rem(x + 4 - 2 * c, 4)
    depth = n_blk // 4

    def place(dz, dx, core):
        at_x = lax.rem(x + dx + 4, 4)
        at_z = lax.rem(z + dz + depth, depth)
        return (at_z * 4 + lax.rem(at_x, 2) * 2 + core, (at_x // 2) * 4 + y)

    def along_y(d):
        return (p, h * 4 + lax.rem(y + d + 4, 4))

    sibling = (p + 1 - 2 * c, g)

    def pick(row):
        a, b, d, e = row
        return jnp.where(role == 0, a, jnp.where(role == 1, b, jnp.where(role == 2, d, e)))

    def look(table, i):
        value = jnp.int32(0)
        for k, row in enumerate(table):
            value = jnp.where(i == k, pick(row), value)
        return value

    def half(ref, k):
        return ref.at[pl.ds(k * chunk, chunk)]

    def remote(src, dst, send, recv, device):
        return pltpu.make_async_remote_copy(
            src_ref=src, dst_ref=dst, send_sem=send, recv_sem=recv, device_id=device, device_id_type=MESH
        )

    rounds = (8, 4, depth)
    seats = (2 * y + c, x, z)

    def peer(r, d):
        seat = lax.rem(seats[r] + d, rounds[r])
        if r == 0:
            return (p - c + lax.rem(seat, 2), h * 4 + seat // 2)
        if r == 1:
            return (z * 4 + lax.rem(seat, 2) * 2 + c, (seat // 2) * 4 + y)
        return (seat * 4 + lax.rem(p, 4), g)

    image_load = pltpu.make_async_copy(image_hbm, image_ref, load_sem.at[0])
    text_load = pltpu.make_async_copy(text_hbm, text_ref, load_sem.at[1])
    image_load.start()
    text_load.start()

    barrier = pltpu.get_barrier_semaphore()
    greeted = [along_y(1), along_y(-1)]
    greeted += [place(dz, dx, core) for dz, dx in ((0, 1), (0, -1), (1, 0), (-1, 0)) for core in (0, 1)]
    greeted += [peer(r, d) for r in range(3) for d in range(1, rounds[r])]
    for device in greeted:
        pl.semaphore_signal(barrier, inc=1, device_id=device, device_id_type=MESH)

    image_load.wait()
    images[c, 0] = normalize(image_ref[...])[0].astype(jnp.bfloat16)
    text_load.wait()
    own_text[...] = normalize(text_ref[...])[0].astype(jnp.bfloat16)

    pl.semaphore_wait(barrier, len(greeted))

    def ring(k):
        slot, part, to, into = ((0, 0, 1, 3), (0, 1, -1, 1), (0, 1, 1, 3), (0, 0, -1, 1), (3, 0, 1, 2), (1, 1, -1, 2))[k]
        return remote(
            half(images.at[c, slot], part), half(images.at[c, into], part),
            ring_send.at[k], ring_recv.at[into, part], along_y(to),
        )

    def ring_arrival(slot, part):
        remote(
            half(images.at[c, slot], part), half(images.at[c, slot], part),
            ring_send.at[0], ring_recv.at[slot, part], sibling,
        ).wait_recv()

    def share(slot):
        return remote(images.at[c, slot], images.at[c, slot], share_send.at[slot], share_recv.at[slot], sibling)

    far = low == 1
    first_hops = (
        (place(0, 0, h), 3 + c, c != h),
        (place(0, jnp.where(far & (c == 1), -1, 1), h), jnp.where(far, 5, 1 + c), None),
        (place(jnp.where(far, 1, 0), jnp.where(far, 0, -1), h), jnp.where(far, jnp.where(c == 0, 5, 0), 1 + c), None),
        (place(1, 0, h), 0, jnp.logical_not(far) & (c == 1)),
    )

    def first(k, part):
        device, into, _ = first_hops[k]
        return remote(
            half(own_text, part), half(texts.at[into], part), first_send.at[k, part], text_recv.at[into, part], device
        )

    hands = (
        (pick((5, 2, 5, 1)), place(0, pick((-1, 1, 1, -1)), c), pick((4, 4, 3, 3))),
        (pick((5, 5, 5, 4)), place(pick((1, 0, 1, 1)), pick((0, -1, 0, 0)), c), pick((2, 1, 1, 0))),
        (pick((0, 0, 4, 4)), place(pick((0, 0, 1, 1)), pick((0, 1, 0, 0)), c), pick((2, 2, 0, 0))),
    )

    def hand(k, part):
        slot, device, into = hands[k]
        return remote(
            half(texts.at[slot], part), half(texts.at[into], part), hand_send.at[k, part], text_recv.at[into, part], device
        )

    def text_arrival(slot, part):
        remote(
            half(own_text, part), half(texts.at[slot], part), first_send.at[0, 0], text_recv.at[slot, part], sibling
        ).wait_recv()

    def when(condition, action):
        if condition is None:
            action()
        else:
            pl.when(condition)(action)

    for part in range(2):
        ring(2 * part).start()
        ring(2 * part + 1).start()
        for k in (1, 2, 3, 0):
            when(first_hops[k][2], lambda k=k, part=part: first(k, part).start())
    share(0).start()

    @pl.when(c == h)
    def _():
        texts[3 + c] = own_text[...]

    parts[pl.ds(5, 2)] = jnp.zeros((2, rows, width), jnp.float32)
    acc[...] = jnp.zeros_like(acc)

    for part in range(2):
        text_arrival(hands[0][0], part)
        hand(0, part).start()

        @pl.when(role == 1)
        def _():
            text_arrival(5, part)

        @pl.when(role < 3)
        def _():
            hand(1, part).start()

        @pl.when(role == 1)
        def _():
            text_arrival(0, part)
            hand(2, part).start()

        if part == 0:
            ring_arrival(3, 0)
            ring(4).start()
            ring_arrival(1, 1)
            ring(5).start()

    ring_arrival(3, 1)
    share(3).start()
    ring_arrival(1, 0)
    share(1).start()
    for part in range(2):

        @pl.when(role >= 2)
        def _():
            text_arrival(4, part)

        @pl.when(role == 2)
        def _():
            hand(2, part).start()

        @pl.when(role == 3)
        def _():
            hand(1, part).start()

    ring_arrival(2, 0)
    ring_arrival(2, 1)
    share(2).start()
    for slot in (0, 1, 3, 2):
        remote(
            images.at[c, slot], images.at[1 - c, slot], share_send.at[slot], share_recv.at[slot], sibling
        ).wait_recv()

    scale = jnp.exp(scale_ref[0])
    offset = bias_ref[0]
    strip = 32
    line = lax.broadcasted_iota(jnp.int32, (strip, rows), 0)
    column = lax.broadcasted_iota(jnp.int32, (strip, rows), 1)

    def fold(values):
        return values.reshape(-1, 8, rows).sum(axis=0)

    def tile(s, lane, into, paired, sums):
        losses, scales, biases = sums
        for k in range(rows // strip):
            lines = pl.ds(k * strip, strip)
            logits = scores[lines, pl.ds(lane, rows)]
            score = scale * logits + offset
            if paired is not None:
                match = (line + k * strip == column) & paired
                score = jnp.where(match, -score, score)
            small = jnp.exp(-jnp.abs(score))
            whole = 1.0 + small
            inverse = 1.0 / whole
            loss = jnp.maximum(score, 0.0) + (jnp.log(whole) + (small - (whole - 1.0)) * inverse)
            slope = jnp.where(score >= 0.0, 1.0, small) * inverse
            if paired is not None:
                slope = jnp.where(match, -slope, slope)
            weights[s, lines, into] = (scale * slope).astype(jnp.bfloat16)
            losses += fold(loss)
            scales += fold(slope * logits)
            biases += fold(slope)
        return losses, scales, biases

    def pairs_of(s, block, tiles, first_lane, paired):
        scores[:, pl.ds(0, tiles * rows)] = dot(texts[s], block, NT)
        sums = (acc[0], acc[1], acc[2])
        for t in range(tiles):
            if isinstance(first_lane, int):
                into = pl.ds(first_lane + t * rows, rows)
            else:
                into = pl.ds(pl.multiple_of(first_lane + t * rows, rows), rows)
            sums = tile(s, t * rows, into, paired if t == 0 else None, sums)
        acc[0], acc[1], acc[2] = sums
        if isinstance(first_lane, int):
            used = weights[s, :, pl.ds(first_lane, tiles * rows)]
        else:
            used = weights[s, :, pl.ds(pl.multiple_of(first_lane, tiles * rows), tiles * rows)]
        parts[s] = dot(used, block, NN)

    strip_rows = 16

    def lines_of(part, i):
        return pl.ds(pl.multiple_of(part * chunk + i * strip_rows, strip_rows), strip_rows)

    def strips(action):
        def body(i, carry):
            action(i)
            return carry

        lax.fori_loop(0, chunk // strip_rows, body, 0, unroll=2)

    def pack(value, wire, into):
        code, step = encode(value)
        wire[into + (pl.ds(0, width),)] = code
        wire[into + (pl.ds(width, 128),)] = jnp.broadcast_to(step, (strip_rows, 128))

    def unpack(wire, at):
        return decode(wire[at + (pl.ds(0, width),)], wire[at + (pl.ds(width, 128),)][:, 0:1])

    def part_copy(i, part):
        core = look(PART_CORE, i)
        device = place(look(PART_Z, i), look(PART_X, i), jnp.where(core == 2, c, core))
        s, into = look(ORDER, i), look(PART_SLOT, i)
        return remote(
            half(wires.at[s], part), half(inbox.at[into], part), part_send.at[i, part], part_recv.at[into, part], device
        )

    def part_sent(i):
        kind = look(SENT, i)
        return (kind == 1) | ((kind == 2) & (c == 1)) | ((kind == 3) & (c == 0))

    def text_step(i, carry):
        s = look(ORDER, i)
        sent = part_sent(i)

        @pl.when(sent)
        def _():
            text_arrival(s, 0)
            text_arrival(s, 1)

        middle = (s > 0) & (s < 4)

        @pl.when(middle)
        def _():
            pairs_of(s, images[...].reshape(8 * rows, width), 8, 0, (c == h) & (s == 3))

        @pl.when(jnp.logical_not(middle))
        def _():
            b = jnp.where(s == 4, 1, 0)
            pairs_of(s, images[b].reshape(4 * rows, width), 4, b * 4 * rows, (c == h) & (s == 4))

        @pl.when(sent)
        def _():
            for part in range(2):

                def code(k):
                    lines = lines_of(part, k)
                    pack(parts[s, lines], wires, (s, lines))

                strips(code)
                part_copy(i, part).start()

        return carry

    lax.fori_loop(0, 5, text_step, 0)

    def image_sum(b, slot):
        lanes = pl.ds(pl.multiple_of((4 * b + slot) * rows, rows), rows)
        lhs = weights[pl.ds(b, 4), :, lanes].reshape(4 * rows, rows)
        rhs = texts[pl.ds(b, 4)].reshape(4 * rows, width)
        return dot(lhs, rhs, TN)

    def core_copy(slot):
        return remote(image_other.at[slot], core_in.at[slot], core_send.at[slot], core_recv.at[slot], sibling)

    def other_step(i, carry):
        slot = lax.rem(i + 2, 4)
        image_other[slot] = image_sum(1 - c, slot)
        core_copy(slot).start()
        return carry

    lax.fori_loop(0, 4, other_step, 0)

    def own_step(i, carry):
        slot = lax.rem(i + 2, 4)
        image_part[slot] = image_sum(c, slot)
        return carry

    lax.fori_loop(0, 4, own_step, 0)

    def back(k):
        slot, part, to, dst, sem = (
            (2, 0, 1, half(relay, 0), relay_recv.at[0]),
            (2, 1, -1, half(relay, 1), relay_recv.at[1]),
            (1, 1, 1, half(image_in.at[0], 1), image_recv.at[0, 1]),
            (3, 0, -1, half(image_in.at[1], 0), image_recv.at[1, 0]),
            (1, 0, 1, half(image_in.at[0], 0), image_recv.at[0, 0]),
            (3, 1, -1, half(image_in.at[1], 1), image_recv.at[1, 1]),
        )[k]
        return remote(half(back_wires.at[slot], part), dst, back_send.at[k], sem, along_y(to))

    def back_start(k, slot, part, add=None):
        def code(i):
            lines = lines_of(part, i)
            value = image_part[slot, lines]
            if add is not None:
                value += unpack(add, (lines,))
            pack(value, back_wires, (slot, lines))

        strips(code)
        back(k).start()

    for slot, ready in ((2, ((0, 0), (1, 1))), (3, ((3, 0),)), (1, ((2, 1),)), (0, ())):
        core_copy(slot).wait_recv()
        image_part[slot] += core_in[slot]
        for k, part in ready:
            back_start(k, slot, part)

    lates = (
        (pick((5, 0, 4, 4)), 0, place(pick((0, -1, 0, 0)), pick((1, 0, -1, 1)), jnp.where(role < 2, 1, c)), pick((4, 5, 2, 0))),
        (pick((5, 5, 5, 1)), pick((1, 1, 2, 1)), place(pick((0, -1, 0, 0)), pick((0, 0, -1, 1)), 0), pick((5, 5, 4, 5))),
        (2, 2, place(0, -1, 1), 4),
    )
    late_on = (None, role > 0, role == 1)

    def late(k, part):
        _, _, device, into = lates[k]
        return remote(
            half(late_wires.at[k], part), half(inbox.at[into], part), late_send.at[k, part], part_recv.at[into, part], device
        )

    def part_arrival(slot, part):
        remote(
            half(inbox.at[slot], part), half(inbox.at[slot], part), late_send.at[0, 0], part_recv.at[slot, part], sibling
        ).wait_recv()

    def absorb(into, slot, part):
        def add(i):
            lines = lines_of(part, i)
            parts[into, lines] += unpack(inbox, (slot, lines))

        strips(add)

    def late_start(k, part):
        into, slot, _, _ = lates[k]

        def add(i):
            lines = lines_of(part, i)
            pack(parts[into, lines] + unpack(inbox, (slot, lines)), late_wires, (k, lines))

        strips(add)
        late(k, part).start()

    def late_0(part):
        @pl.when(role == 0)
        def _():
            part_arrival(1, part)
            absorb(5, 1, part)

        part_arrival(0, part)
        late_start(0, part)

    def late_1(part):
        part_arrival(1, part)

        @pl.when(role == 2)
        def _():
            absorb(5, 1, part)
            part_arrival(2, part)

        late_start(1, part)

    def late_2(part):
        part_arrival(2, part)
        late_start(2, part)

    def total_copy(r, d):
        seat = seats[r]
        return remote(
            totals.at[r, seat], totals.at[r, seat], total_send.at[r, d - 1], total_recv.at[r, seat], peer(r, d)
        )

    def total_sum(r):
        for d in range(1, rounds[r]):
            seat = lax.rem(seats[r] + d, rounds[r])
            remote(
                totals.at[r, seat], totals.at[r, seat], total_send.at[r, d - 1], total_recv.at[r, seat], sibling
            ).wait_recv()
        value = totals[r, 0]
        for seat in range(1, rounds[r]):
            value += totals[r, seat]
        return value

    def total_start(r, value):
        totals[r, seats[r]] = value
        for d in range(1, rounds[r]):
            total_copy(r, d).start()

    def relayed(k):
        slot, part = ((1, 0), (3, 1))[k]
        remote(half(relay, k), half(relay, k), back_send.at[0], relay_recv.at[k], sibling).wait_recv()
        back_start(4 + k, slot, part, relay)

    total_start(0, jnp.concatenate([jnp.sum(acc[k], axis=0, keepdims=True)[None] for k in range(3)], axis=0))
    pl.when(role == 1)(lambda: late_1(0))
    pl.when(role > 1)(lambda: late_0(0))
    pl.when(role == 1)(lambda: late_1(1))
    pl.when(role > 1)(lambda: late_0(1))
    total_start(1, total_sum(0))
    pl.when(role == 1)(lambda: late_0(0))
    pl.when(role > 1)(lambda: late_1(0))
    relayed(0)
    relayed(1)
    total_start(2, total_sum(1))
    pl.when(role == 1)(lambda: late_0(1))
    pl.when(role > 1)(lambda: late_1(1))
    pl.when(role == 0)(lambda: late_0(0))
    pl.when(role == 1)(lambda: late_2(0))
    pl.when(role == 0)(lambda: late_0(1))
    pl.when(role == 1)(lambda: late_2(1))
    total = jnp.sum(total_sum(2), axis=-1, keepdims=True)
    pairs = float(n_blk * n_grp * rows * STEPS * n_grp * rows)
    sums_ref[0:1, :] = jnp.broadcast_to(total[0] / pairs, (1, 128))
    sums_ref[1:2, :] = jnp.broadcast_to(total[1] * scale / pairs, (1, 128))
    sums_ref[2:3, :] = jnp.broadcast_to(total[2] / pairs, (1, 128))

    for part in range(2):
        for slot in range(2):
            remote(
                half(image_in.at[slot], part), half(image_in.at[slot], part),
                back_send.at[0], image_recv.at[slot, part], sibling,
            ).wait_recv()

        def last(i):
            lines = lines_of(part, i)
            total = image_part[0, lines] + unpack(image_in, (0, lines)) + unpack(image_in, (1, lines))
            grad_image_ref[lines] = finish(image_ref[lines], total)

        strips(last)

    extra = jnp.logical_not(far) & (c == 1)
    own = jnp.where(c == h, 3 + c, 6)
    for part in range(2):

        @pl.when(c != h)
        def _():
            part_arrival(3, part)
            absorb(6, 3, part)

        part_arrival(4, part)

        @pl.when(extra)
        def _():
            part_arrival(6, part)
            absorb(own, 6, part)

        part_arrival(5, part)

        def last(i):
            lines = lines_of(part, i)
            total = parts[own, lines] + unpack(inbox, (4, lines)) + unpack(inbox, (5, lines))
            grad_text_ref[lines] = finish(text_ref[lines], total)

        strips(last)

    for k in range(6):
        ring(k).wait_send()
        back(k).wait_send()
    for slot in range(4):
        share(slot).wait_send()
        core_copy(slot).wait_send()
    for part in range(2):
        for k in range(4):
            when(first_hops[k][2], lambda k=k, part=part: first(k, part).wait_send())
        hand(0, part).wait_send()
        hand(1, part).wait_send()
        pl.when((role == 1) | (role == 2))(lambda part=part: hand(2, part).wait_send())
        for k in range(3):
            when(late_on[k], lambda k=k, part=part: late(k, part).wait_send())

    def drain(i, carry):
        @pl.when(part_sent(i))
        def _():
            part_copy(i, 0).wait_send()
            part_copy(i, 1).wait_send()

        return carry

    lax.fori_loop(0, 5, drain, 0)
    for r in range(3):
        for d in range(1, rounds[r]):
            total_copy(r, d).wait_send()


def local(n_blk, n_grp, image_embed, text_embed, log_scale, bias):
    rows, width = image_embed.shape
    low, wide = jnp.bfloat16, jnp.float32
    dma = pltpu.SemaphoreType.DMA
    vmem = pl.BlockSpec(memory_space=pltpu.VMEM)
    smem = pl.BlockSpec(memory_space=pltpu.SMEM)
    hbm = pl.BlockSpec(memory_space=pltpu.HBM)
    out = jax.ShapeDtypeStruct((rows, width), wide)
    pairs = n_grp * rows * STEPS * rows
    grad_image, grad_text, sums = pl.pallas_call(
        functools.partial(kernel, n_blk, n_grp),
        out_shape=(out, out, jax.ShapeDtypeStruct((8, 128), wide)),
        in_specs=[smem, smem, hbm, hbm],
        out_specs=(vmem, vmem, vmem),
        scratch_shapes=[
            pltpu.VMEM((rows, width), low),
            pltpu.VMEM((rows, width), low),
            dma((2,)),
            pltpu.VMEM((2, 4, rows, width), low),
            pltpu.VMEM((6, rows, width), low),
            pltpu.VMEM((rows, width), low),
            pltpu.VMEM((rows, 8 * rows), wide),
            pltpu.VMEM((5, rows, 8 * rows), low),
            pltpu.VMEM((7, rows, width), wide),
            pltpu.VMEM((5, rows, width + 128), low),
            pltpu.VMEM((7, rows, width + 128), low),
            pltpu.VMEM((3, rows, width + 128), low),
            pltpu.VMEM((4, rows, width), wide),
            pltpu.VMEM((4, rows, width), wide),
            pltpu.VMEM((4, rows, width), wide),
            pltpu.VMEM((4, rows, width + 128), low),
            pltpu.VMEM((rows, width + 128), low),
            pltpu.VMEM((2, rows, width + 128), low),
            pltpu.VMEM((3, 8, 128), wide),
            pltpu.VMEM((3, 8, 3, 1, 128), wide),
            dma((6,)), dma((4, 2)), dma((4,)), dma((4,)), dma((4, 2)), dma((3, 2)), dma((6, 2)),
            dma((5, 2)), dma((3, 2)), dma((7, 2)), dma((4,)), dma((4,)), dma((6,)), dma((2,)), dma((2, 2)),
            dma((3, 8)), dma((3, 8)),
        ],
        compiler_params=pltpu.CompilerParams(
            collective_id=0, has_side_effects=True, vmem_limit_bytes=48 << 20
        ),
        cost_estimate=pl.CostEstimate(
            flops=6 * pairs * width, bytes_accessed=12 * rows * width, transcendentals=3 * pairs
        ),
        name="pair_loss",
    )(log_scale, bias, image_embed, text_embed)
    return grad_image, grad_text, sums[0, 0], sums[1, 0], sums[2, 0]


def solution(mesh):
    split = P(("blk", "grp"), None)
    return jax.shard_map(
        functools.partial(local, mesh.shape["blk"], mesh.shape["grp"]),
        mesh=mesh,
        in_specs=(split, split, P(), P()),
        out_specs=(split, split, P(), P(), P()),
        check_vma=False,
    )
```

time: 539 us -> 66.6 us (0.12)
  waiting for transfers between devices: 376 us -> 0 us
  blocking collectives: 73.7 us -> 0 us
  Pallas kernels: 0 us -> 60.4 us
  matrix products: 32 us -> 0 us
  between operations: 28.3 us -> 1.94 us
  other arithmetic: 16.2 us -> 0 us
  starting transfers between devices: 12.1 us -> 0 us
    ppermute x7 -> x0, waiting for transfers between devices: 229 us -> none  [shifted(): return lax.ppermute(block, axis, route)]
    reduce_scatter x1 -> x0, waiting for transfers between devices: 84.1 us -> none  [local(): finished = lax.psum_scatter(carried, 'grp', scatter_dimension=0, tiled=True)]
    psum x1 -> x0, blocking collectives: 73.7 us -> none  [local(): lax.psum((loss_sum, scale_sum, bias_sum), ('blk', 'grp'))]
    all_gather x1 -> x0, waiting for transfers between devices: 63 us -> none  [local(): texts = lax.all_gather(text_low, 'grp', axis=0, tiled=True)]
    pallas_call x0 -> x1, Pallas kernels: none -> 60.4 us  [local(): pl.pallas_call(functools.partial(kernel, n_blk, n_grp), out_shape=(out, o...]
    dot_general x12 -> x0, matrix products: 32 us -> none  [the longest x4 13.3 us: local(): lax.dot_general(image_low, texts, (((1,), (1,)), ((), ())), preferred_ele...]
    ppermute x7 -> x0, starting transfers between devices: 12 us -> none  [shifted(): return lax.ppermute(block, axis, route)]
    add x7 -> x0, other arithmetic: 9.86 us -> none  [the longest x2 9.84 us: local(): carried = carried + text_side(weights, image_low)]
  transfers between devices with their start and end apart: 9 -> 0, of which waited for: 5 -> 0; matrix products, arithmetic and copies ran while one was open for 4% -> 0% of each run, Pallas kernels for 0% -> 0%
where the time goes in v2:
time: 66.6 us; the launch traced here: 66.5 us
  Pallas kernels  60.4 us (91%)
  local copies, waits for them, and re-layouts  4.07 us (6%)
  between operations  1.94 us (3%)
    pallas_call x1, Pallas kernels, local(): pl.pallas_call(functools.partial(kernel, n_blk, n_grp), out_shape=(out, o...  60.4 us
    unnamed x6, local copies, waits for them, and re-layouts  3.54 us

profile of v2, /device:TPU:1, one launch (start us, length us, event | category | flops | bytes accessed | tf_op | source)
XLA Modules:
  0.0 66.5 jit_solution(6139695582738854858)
XLA Ops:
  1.9 0.0 copy-start
  1.9 1.0 %copy-done = bf16[128,1152]{1,0:T(8,128)(2,1)S(1)} copy-done((bf16[128,1152]{1,0:T(8,128)(2,1)S(1)}, bf16[128,1152]{1,0:T(8,128)(2,1)}, u32[]{:S(2)}) %copy-start) | copy-done | bytes 294936
  2.9 0.0 copy-start.1
  2.9 1.0 %copy-done.1 = bf16[128,1152]{1,0:T(8,128)(2,1)S(1)} copy-done((bf16[128,1152]{1,0:T(8,128)(2,1)S(1)}, bf16[128,1152]{1,0:T(8,128)(2,1)}, u32[]{:S(2)}) %copy-start.1) | copy-done | bytes 294936
  3.8 60.4 %pair_loss.1 = (f32[128,1152]{1,0:T(8,128)S(1)}, f32[128,1152]{1,0:T(8,128)S(1)}, f32[8,128]{1,0:T(8,128)S(1)}) custom-call(f32[1]{0:T(128)S(6)} %copy.11.scale_ref, f32[1]{0:T(128)S(6)} %copy.12.bias_ref, bf16[128,1152]{1,0:T(8,128)(2,1)S(1)} %copy-done, bf16[128,1152]{1,0:T(8,128)(2,1)S(1)} %copy-done.1), custom_call_target="tpu_custom_call" | custom-call | flops 3623878656 | bytes 1769472 | tf_op jit(solution)/shard_map/pair_loss/pallas_call | solution.py:607
  64.3 0.5 fusion
  64.8 0.8 %copy.13 = f32[128,1152]{1,0:T(8,128)} copy(f32[128,1152]{1,0:T(8,128)S(1)} %get-tuple-element.19) | data formatting | bytes 1179648
  65.6 0.8 %copy.14 = f32[128,1152]{1,0:T(8,128)} copy(f32[128,1152]{1,0:T(8,128)S(1)} %get-tuple-element.20) | data formatting | bytes 1179648
Async XLA Ops:
  1.9 1.0 %copy-start = (bf16[128,1152]{1,0:T(8,128)(2,1)S(1)}, bf16[128,1152]{1,0:T(8,128)(2,1)}, u32[]{:S(2)}) copy-start(bf16[128,1152]{1,0:T(8,128)(2,1)} %image_hbm.1) | copy-start | bytes 884740
  2.9 1.0 %copy-start.1 = (bf16[128,1152]{1,0:T(8,128)(2,1)S(1)}, bf16[128,1152]{1,0:T(8,128)(2,1)}, u32[]{:S(2)}) copy-start(bf16[128,1152]{1,0:T(8,128)(2,1)} %text_hbm.1) | copy-start | bytes 884740

commit v3 on v2

--- a/solution.py
+++ b/solution.py
@@ -14,11 +14,11 @@
 TN = (((0,), (0,)), ((), ()))
 NN = (((1,), (0,)), ((), ()))
 
-ORDER = ((2, 1, 0, 3), (1, 0, 1, 0), (0, 2, 3, 2), (3, 3, 2, 4), (4, 4, 4, 1))
-PART_Z = ((-1, 0, -1, 0), (0, 0, -1, -1), (-1, 0, 0, 0), (0, 0, 0, 0), (0, 0, 0, 0))
-PART_X = ((0, -1, 0, -1), (1, 0, 0, 0), (0, 0, 1, 1), (0, 0, -1, 0), (0, 0, 0, 0))
-PART_CORE = ((2, 0, 2, 2), (2, 2, 2, 2), (1, 2, 2, 1), (0, 0, 2, 2), (1, 1, 2, 2))
-PART_SLOT = ((1, 4, 0, 2), (1, 0, 1, 0), (6, 0, 1, 5), (3, 3, 0, 0), (3, 3, 0, 0))
+ORDER = ((2, 1, 1, 3), (1, 0, 3, 2), (0, 2, 2, 0), (3, 3, 0, 4), (4, 4, 4, 1))
+PART_Z = ((-1, 0, -1, 0), (0, 0, 0, 0), (-1, 0, 0, -1), (0, 0, -1, 0), (0, 0, 0, 0))
+PART_X = ((0, -1, 0, -1), (1, 0, 1, 1), (0, 0, -1, 0), (0, 0, 0, 0), (0, 0, 0, 0))
+PART_CORE = ((2, 0, 2, 2), (2, 2, 2, 1), (1, 2, 2, 2), (0, 0, 2, 2), (1, 1, 2, 2))
+PART_SLOT = ((1, 4, 1, 2), (1, 0, 1, 5), (6, 0, 0, 0), (3, 3, 0, 0), (3, 3, 0, 0))
 SENT = ((1, 1, 1, 1), (1, 0, 1, 1), (1, 0, 1, 1), (2, 2, 1, 0), (3, 3, 0, 0))
 
 
@@ -300,7 +300,7 @@
             used = weights[s, :, pl.ds(pl.multiple_of(first_lane, tiles * rows), tiles * rows)]
         parts[s] = dot(used, block, NN)
 
-    strip_rows = 16
+    strip_rows = 32
 
     def lines_of(part, i):
         return pl.ds(pl.multiple_of(part * chunk + i * strip_rows, strip_rows), strip_rows)
@@ -367,6 +367,30 @@
 
     lax.fori_loop(0, 5, text_step, 0)
 
+    def total_copy(r, d):
+        seat = seats[r]
+        return remote(
+            totals.at[r, seat], totals.at[r, seat], total_send.at[r, d - 1], total_recv.at[r, seat], peer(r, d)
+        )
+
+    def total_sum(r):
+        for d in range(1, rounds[r]):
+            seat = lax.rem(seats[r] + d, rounds[r])
+            remote(
+                totals.at[r, seat], totals.at[r, seat], total_send.at[r, d - 1], total_recv.at[r, seat], sibling
+            ).wait_recv()
+        value = totals[r, 0]
+        for seat in range(1, rounds[r]):
+            value += totals[r, seat]
+        return value
+
+    def total_start(r, value):
+        totals[r, seats[r]] = value
+        for d in range(1, rounds[r]):
+            total_copy(r, d).start()
+
+    total_start(0, jnp.concatenate([jnp.sum(acc[k], axis=0, keepdims=True)[None] for k in range(3)], axis=0))
+
     def image_sum(b, slot):
         lanes = pl.ds(pl.multiple_of((4 * b + slot) * rows, rows), rows)
         lhs = weights[pl.ds(b, 4), :, lanes].reshape(4 * rows, rows)
@@ -377,7 +401,7 @@
         return remote(image_other.at[slot], core_in.at[slot], core_send.at[slot], core_recv.at[slot], sibling)
 
     def other_step(i, carry):
-        slot = lax.rem(i + 2, 4)
+        slot = jnp.where(i < 2, 2 + i, 3 - i)
         image_other[slot] = image_sum(1 - c, slot)
         core_copy(slot).start()
         return carry
@@ -385,11 +409,12 @@
     lax.fori_loop(0, 4, other_step, 0)
 
     def own_step(i, carry):
-        slot = lax.rem(i + 2, 4)
+        slot = jnp.where(i < 2, 2 + i, 3 - i)
         image_part[slot] = image_sum(c, slot)
         return carry
 
     lax.fori_loop(0, 4, own_step, 0)
+    total_start(1, total_sum(0))
 
     def back(k):
         slot, part, to, dst, sem = (
@@ -477,44 +502,20 @@
         part_arrival(2, part)
         late_start(2, part)
 
-    def total_copy(r, d):
-        seat = seats[r]
-        return remote(
-            totals.at[r, seat], totals.at[r, seat], total_send.at[r, d - 1], total_recv.at[r, seat], peer(r, d)
-        )
-
-    def total_sum(r):
-        for d in range(1, rounds[r]):
-            seat = lax.rem(seats[r] + d, rounds[r])
-            remote(
-                totals.at[r, seat], totals.at[r, seat], total_send.at[r, d - 1], total_recv.at[r, seat], sibling
-            ).wait_recv()
-        value = totals[r, 0]
-        for seat in range(1, rounds[r]):
-            value += totals[r, seat]
-        return value
-
-    def total_start(r, value):
-        totals[r, seats[r]] = value
-        for d in range(1, rounds[r]):
-            total_copy(r, d).start()
-
     def relayed(k):
         slot, part = ((1, 0), (3, 1))[k]
         remote(half(relay, k), half(relay, k), back_send.at[0], relay_recv.at[k], sibling).wait_recv()
         back_start(4 + k, slot, part, relay)
 
-    total_start(0, jnp.concatenate([jnp.sum(acc[k], axis=0, keepdims=True)[None] for k in range(3)], axis=0))
     pl.when(role == 1)(lambda: late_1(0))
     pl.when(role > 1)(lambda: late_0(0))
     pl.when(role == 1)(lambda: late_1(1))
     pl.when(role > 1)(lambda: late_0(1))
-    total_start(1, total_sum(0))
+    total_start(2, total_sum(1))
     pl.when(role == 1)(lambda: late_0(0))
     pl.when(role > 1)(lambda: late_1(0))
     relayed(0)
     relayed(1)
-    total_start(2, total_sum(1))
     pl.when(role == 1)(lambda: late_0(1))
     pl.when(role > 1)(lambda: late_1(1))
     pl.when(role == 0)(lambda: late_0(0))
@@ -641,7 +642,11 @@
             flops=6 * pairs * width, bytes_accessed=12 * rows * width, transcendentals=3 * pairs
         ),
         name="pair_loss",
-    )(log_scale, bias, image_embed, text_embed)
+    )(
+        log_scale, bias,
+        pltpu.with_memory_space_constraint(image_embed, pltpu.HBM),
+        pltpu.with_memory_space_constraint(text_embed, pltpu.HBM),
+    )
     return grad_image, grad_text, sums[0, 0], sums[1, 0], sums[2, 0]
 
 

time: 66.6 us -> 56.9 us (0.85)
  Pallas kernels: 60.4 us -> 52.7 us
  local copies, waits for them, and re-layouts: 4.07 us -> 2.15 us
    pallas_call x1, Pallas kernels: 60.4 us -> 52.7 us  [local(): pl.pallas_call(functools.partial(kernel, n_blk, n_grp), out_shape=(out, o...]
    unnamed x6 -> x2, local copies, waits for them, and re-layouts: 3.54 us -> 1.63 us
where the time goes in v3:
time: 56.9 us; the launch traced here: 56.8 us
  Pallas kernels  52.7 us (93%)
  local copies, waits for them, and re-layouts  2.15 us (4%)
  between operations  1.93 us (3%)
    pallas_call x1, Pallas kernels, local(): pl.pallas_call(functools.partial(kernel, n_blk, n_grp), out_shape=(out, o...  52.7 us
    unnamed x2, local copies, waits for them, and re-layouts  1.63 us

profile of v3, /device:TPU:1, one launch (start us, length us, event | category | flops | bytes accessed | tf_op | source)
XLA Modules:
  0.0 56.8 jit_solution(15344770881613542804)
XLA Ops:
  1.9 52.7 %pair_loss.1 = (f32[128,1152]{1,0:T(8,128)S(1)}, f32[128,1152]{1,0:T(8,128)S(1)}, f32[8,128]{1,0:T(8,128)S(1)}) custom-call(f32[1]{0:T(128)S(6)} %copy.11.scale_ref, f32[1]{0:T(128)S(6)} %copy.12.bias_ref, bf16[128,1152]{1,0:T(8,128)(2,1)} %image_hbm.1, bf16[128,1152]{1,0:T(8,128)(2,1)} %text_hbm.1), custom_call_target="tpu_custom_call" | custom-call | flops 3623878656 | bytes 1769472 | tf_op jit(solution)/shard_map/pair_loss/pallas_call | solution.py:608
  54.6 0.5 fusion
  55.2 0.8 %copy.13 = f32[128,1152]{1,0:T(8,128)} copy(f32[128,1152]{1,0:T(8,128)S(1)} %get-tuple-element.19) | data formatting | bytes 1179648
  56.0 0.8 %copy.14 = f32[128,1152]{1,0:T(8,128)} copy(f32[128,1152]{1,0:T(8,128)S(1)} %get-tuple-element.20) | data formatting | bytes 1179648

commit v4 on v3

--- a/solution.py
+++ b/solution.py
@@ -36,20 +36,18 @@
 def encode(value):
     top = jnp.max(jnp.abs(value), axis=1, keepdims=True)
     step = (jnp.maximum(top, 1e-30) * (1.008 / 16383.0)).astype(jnp.bfloat16).astype(jnp.float32)
-    whole = (value * (1.0 / step) + ROUND) - ROUND
-    upper = jnp.floor(whole * (1.0 / 128.0))
-    lower = whole - 128.0 * upper
-    signed = jnp.where(upper >= 0.0, upper + 128.0, upper - 127.0)
-    return (signed * jnp.exp2(lower - 71.0)).astype(jnp.bfloat16), step.astype(jnp.bfloat16)
+    scaled = value * ((1.0 / 128.0) / step)
+    upper = jnp.floor(scaled)
+    power = ((scaled - upper) * 128.0 + (ROUND - 71.0)) - ROUND
+    signed = upper + jnp.where(upper >= 0.0, 128.0, -127.0)
+    return (signed * jnp.exp2(power)).astype(jnp.bfloat16), step.astype(jnp.bfloat16)
 
 
 def decode(code, step):
     wide = code.astype(jnp.float32)
-    size = jnp.abs(wide)
-    power = jnp.floor(jnp.log2(size) + 0.001)
-    mantissa = size * jnp.exp2(7.0 - power)
-    upper = jnp.where(wide >= 0.0, mantissa - 128.0, 127.0 - mantissa)
-    return (upper * 128.0 + (power + 64.0)) * step.astype(jnp.float32)
+    power = jnp.floor(jnp.log2(jnp.abs(wide)) + 0.001)
+    upper = wide * jnp.exp2(14.0 - power) + jnp.where(wide >= 0.0, -16320.0, 16320.0)
+    return (upper + power) * step.astype(jnp.float32)
 
 
 def dot(a, b, dims):
@@ -135,6 +133,9 @@
     text_load.wait()
     own_text[...] = normalize(text_ref[...])[0].astype(jnp.bfloat16)
 
+    parts[pl.ds(5, 2)] = jnp.zeros((2, rows, width), jnp.float32)
+    acc[...] = jnp.zeros_like(acc)
+
     pl.semaphore_wait(barrier, len(greeted))
 
     def ring(k):
@@ -201,8 +202,6 @@
     def _():
         texts[3 + c] = own_text[...]
 
-    parts[pl.ds(5, 2)] = jnp.zeros((2, rows, width), jnp.float32)
-    acc[...] = jnp.zeros_like(acc)
 
     for part in range(2):
         text_arrival(hands[0][0], part)

time: 56.9 us -> 56.3 us (0.989)
  Pallas kernels: 52.7 us -> 52.1 us
    pallas_call x1, Pallas kernels: 52.7 us -> 52.1 us  [local(): pl.pallas_call(functools.partial(kernel, n_blk, n_grp), out_shape=(out, o...]
where the time goes in v4:
time: 56.3 us; the launch traced here: 56.2 us
  Pallas kernels  52.1 us (93%)
  local copies, waits for them, and re-layouts  2.15 us (4%)
  between operations  1.93 us (3%)
    pallas_call x1, Pallas kernels, local(): pl.pallas_call(functools.partial(kernel, n_blk, n_grp), out_shape=(out, o...  52.1 us
    unnamed x2, local copies, waits for them, and re-layouts  1.63 us

profile of v4, /device:TPU:1, one launch (start us, length us, event | category | flops | bytes accessed | tf_op | source)
XLA Modules:
  0.0 56.2 jit_solution(5426215542192914838)
XLA Ops:
  1.9 52.1 %pair_loss.1 = (f32[128,1152]{1,0:T(8,128)S(1)}, f32[128,1152]{1,0:T(8,128)S(1)}, f32[8,128]{1,0:T(8,128)S(1)}) custom-call(f32[1]{0:T(128)S(6)} %copy.11.scale_ref, f32[1]{0:T(128)S(6)} %copy.12.bias_ref, bf16[128,1152]{1,0:T(8,128)(2,1)} %image_hbm.1, bf16[128,1152]{1,0:T(8,128)(2,1)} %text_hbm.1), custom_call_target="tpu_custom_call" | custom-call | flops 3623878656 | bytes 1769472 | tf_op jit(solution)/shard_map/pair_loss/pallas_call | solution.py:607
  54.0 0.5 fusion
  54.5 0.8 %copy.13 = f32[128,1152]{1,0:T(8,128)} copy(f32[128,1152]{1,0:T(8,128)S(1)} %get-tuple-element.19) | data formatting | bytes 1179648
  55.3 0.8 %copy.14 = f32[128,1152]{1,0:T(8,128)} copy(f32[128,1152]{1,0:T(8,128)S(1)} %get-tuple-element.20) | data formatting | bytes 1179648

commit v5 on v4

--- a/solution.py
+++ b/solution.py
@@ -14,11 +14,11 @@
 TN = (((0,), (0,)), ((), ()))
 NN = (((1,), (0,)), ((), ()))
 
-ORDER = ((2, 1, 1, 3), (1, 0, 3, 2), (0, 2, 2, 0), (3, 3, 0, 4), (4, 4, 4, 1))
+ORDER = ((2, 1, 1, 2), (1, 0, 3, 3), (0, 2, 2, 0), (3, 3, 0, 4), (4, 4, 4, 1))
 PART_Z = ((-1, 0, -1, 0), (0, 0, 0, 0), (-1, 0, 0, -1), (0, 0, -1, 0), (0, 0, 0, 0))
-PART_X = ((0, -1, 0, -1), (1, 0, 1, 1), (0, 0, -1, 0), (0, 0, 0, 0), (0, 0, 0, 0))
-PART_CORE = ((2, 0, 2, 2), (2, 2, 2, 1), (1, 2, 2, 2), (0, 0, 2, 2), (1, 1, 2, 2))
-PART_SLOT = ((1, 4, 1, 2), (1, 0, 1, 5), (6, 0, 0, 0), (3, 3, 0, 0), (3, 3, 0, 0))
+PART_X = ((0, -1, 0, 1), (1, 0, 1, -1), (0, 0, -1, 0), (0, 0, 0, 0), (0, 0, 0, 0))
+PART_CORE = ((2, 0, 2, 1), (2, 2, 2, 2), (1, 2, 2, 2), (0, 0, 2, 2), (1, 1, 2, 2))
+PART_SLOT = ((1, 4, 1, 5), (1, 0, 1, 2), (6, 0, 0, 0), (3, 3, 0, 0), (3, 3, 0, 0))
 SENT = ((1, 1, 1, 1), (1, 0, 1, 1), (1, 0, 1, 1), (2, 2, 1, 0), (3, 3, 0, 0))
 
 

time: 56.3 us -> 56.3 us (level)
  no operation moved by 1% of the time
where the time goes in v5:
time: 56.3 us; the launch traced here: 56.2 us
  Pallas kernels  52.1 us (93%)
  local copies, waits for them, and re-layouts  2.15 us (4%)
  between operations  1.93 us (3%)
    pallas_call x1, Pallas kernels, local(): pl.pallas_call(functools.partial(kernel, n_blk, n_grp), out_shape=(out, o...  52.1 us
    unnamed x2, local copies, waits for them, and re-layouts  1.63 us

profile of v5, /device:TPU:1, one launch (start us, length us, event | category | flops | bytes accessed | tf_op | source)
XLA Modules:
  0.0 56.2 jit_solution(17131291150275977610)
XLA Ops:
  1.9 52.1 %pair_loss.1 = (f32[128,1152]{1,0:T(8,128)S(1)}, f32[128,1152]{1,0:T(8,128)S(1)}, f32[8,128]{1,0:T(8,128)S(1)}) custom-call(f32[1]{0:T(128)S(6)} %copy.11.scale_ref, f32[1]{0:T(128)S(6)} %copy.12.bias_ref, bf16[128,1152]{1,0:T(8,128)(2,1)} %image_hbm.1, bf16[128,1152]{1,0:T(8,128)(2,1)} %text_hbm.1), custom_call_target="tpu_custom_call" | custom-call | flops 3623878656 | bytes 1769472 | tf_op jit(solution)/shard_map/pair_loss/pallas_call | solution.py:607
  54.0 0.5 fusion
  54.5 0.8 %copy.13 = f32[128,1152]{1,0:T(8,128)} copy(f32[128,1152]{1,0:T(8,128)S(1)} %get-tuple-element.19) | data formatting | bytes 1179648
  55.4 0.8 %copy.14 = f32[128,1152]{1,0:T(8,128)} copy(f32[128,1152]{1,0:T(8,128)S(1)} %get-tuple-element.20) | data formatting | bytes 1179648
